TPU v7x, 32 devices: a whole 2x2x4 slice. The times are simulated.
32 devices in a mesh: dom: 32 (over z, y, x, core).
Axes of the slice: x: 2, y: 2, z: 4, core: 2. Of those that a mesh axis runs over, the one named last changes fastest.
Arguments:
- features: bfloat16 [16384, 768], P('dom'), may hold values from -6 to 6
- w_self: bfloat16 [768, 1024], replicated, may hold values from -0.21875 to 0.21875
- w_neigh: bfloat16 [768, 1024], replicated, may hold values from -0.21875 to 0.21875
- tile_cols: int32 [128, 6], P('dom'), may hold values from 0 to 6
- tile_weights: int32 [128, 6, 128, 128], P('dom'), may hold values from 0 to 3
- send_rows: int32 [32, 32, 32], P('dom'), may hold values from 0 to 511
- send_counts: int32 [32, 32], P('dom'), may hold values from 0 to 32, as said below
- hub_rows: int32 [32, 4], P('dom'), may hold values from 0 to 511
- readers: int32 [32, 128], P('dom'), may hold values 0 or 1
- cotangent: bfloat16 [16384, 1024], P('dom'), may hold values from -6 to 6
Outputs:
- out_rows: bfloat16 [16384, 1024], P('dom')
- grad_features: bfloat16 [16384, 768], P('dom')
- grad_self: float32 [768, 1024], replicated
- grad_neigh: float32 [768, 1024], replicated
Inputs may be any that keep to these rules, and one draw needn't show every extreme that they name: send_counts[s, p] is the number of live leading slots of send_rows[s, p]; it is 0 for p == s and wherever (p - s) modulo 32 is neither within 1 to 4 nor within 28 to 31; for every s, send_counts[s, (s + 1) modulo 32] equals 32.
All inputs are finite; a program needn't handle non-finite values. No bound on the sum of `readers` on one device may be relied on, other than what follows from the above.
Results may differ from a plain program's by a relative error of at most 0.0054.
Values may be sent and summed in bfloat16 or wider, within the bound.
A program may use at most 192 MiB of HBM per device.

v0:
```python
import jax
import jax.numpy as jnp
from jax import lax
from jax.sharding import PartitionSpec as P

REACH = 4


def shifted(array, axis, by):
    length = lax.axis_size(axis)
    return lax.ppermute(array, axis, [(i, (i + by) % length) for i in range(length)])


def near_offsets(reach):
    return list(range(1, reach + 1)) + [-distance for distance in range(1, reach + 1)]


def on_device(
    features,
    w_self,
    w_neigh,
    tile_cols,
    tile_weights,
    send_rows,
    send_counts,
    hub_rows,
    readers,
    cotangent,
):
    peers = lax.axis_size("dom")
    own_index = lax.axis_index("dom")
    rows, width = features.shape
    slots = send_rows.shape[2]
    tile = tile_weights.shape[2]
    row_blocks = tile_weights.shape[0]
    offsets = near_offsets(REACH)
    targets = send_rows[0]
    live = jnp.arange(slots, dtype=jnp.int32)[None, :] < send_counts[0][:, None]
    outgoing = features[targets] * live[:, :, None].astype(jnp.bfloat16)
    arrivals = []
    for offset in offsets:
        piece = lax.dynamic_index_in_dim(outgoing, (own_index + offset) % peers, 0, keepdims=False)
        arrivals.append(shifted(piece, "dom", offset))
    halo = jnp.stack(arrivals, axis=0)
    own_hubs = features[hub_rows[0]]
    all_hubs = lax.all_gather(own_hubs, "dom", axis=0, tiled=True)
    flag = readers[0]
    stacked = jnp.concatenate(
        [features, halo.reshape(-1, width), all_hubs * flag[:, None].astype(jnp.bfloat16)], axis=0
    )
    blocks = stacked.reshape(-1, tile, width)
    picked = blocks[tile_cols]
    weights = tile_weights.astype(jnp.bfloat16)
    total = jnp.einsum("rkij,rkjf->rif", weights, picked, preferred_element_type=jnp.float32)
    inverse = 1.0 / (jnp.sum(tile_weights, axis=(1, 3)).astype(jnp.float32) + 1.0)
    neigh = (total * inverse[:, :, None]).reshape(rows, width).astype(jnp.bfloat16)
    pre = jnp.dot(features, w_self, preferred_element_type=jnp.float32) + jnp.dot(
        neigh, w_neigh, preferred_element_type=jnp.float32
    )
    out_rows = jax.nn.silu(pre).astype(jnp.bfloat16)
    sigma = jax.nn.sigmoid(pre)
    dpre = (cotangent.astype(jnp.float32) * sigma * (1.0 + pre * (1.0 - sigma))).astype(
        jnp.bfloat16
    )
    first_dims = (((0,), (0,)), ((), ()))
    term_self = lax.dot_general(features, dpre, first_dims, preferred_element_type=jnp.float32)
    term_neigh = lax.dot_general(neigh, dpre, first_dims, preferred_element_type=jnp.float32)
    grad_self, grad_neigh = lax.psum((term_self, term_neigh), "dom")
    second_dims = (((1,), (1,)), ((), ()))
    grad = lax.dot_general(dpre, w_self, second_dims, preferred_element_type=jnp.float32)
    middle = lax.dot_general(dpre, w_neigh, second_dims, preferred_element_type=jnp.float32)
    scaled = (middle.reshape(row_blocks, tile, width) * inverse[:, :, None]).astype(jnp.bfloat16)
    contrib = jnp.einsum("rkij,rif->rkjf", weights, scaled, preferred_element_type=jnp.float32)
    col_blocks = blocks.shape[0]
    onehot = (jnp.arange(col_blocks, dtype=jnp.int32)[:, None] == tile_cols.reshape(1, -1)).astype(
        jnp.float32
    )
    spread = jnp.dot(
        onehot,
        contrib.reshape(-1, tile * width),
        precision=lax.Precision.HIGHEST,
        preferred_element_type=jnp.float32,
    ).reshape(-1, width)
    halo_count = len(offsets) * slots
    grad = grad + spread[:rows]
    halo_grad = spread[rows : rows + halo_count].reshape(len(offsets), slots, width)
    hub_grad = spread[rows + halo_count :] * flag[:, None].astype(jnp.float32)
    returned = jnp.zeros((peers, slots, width), jnp.float32)
    for position, offset in enumerate(offsets):
        arrived = shifted(halo_grad[position].astype(jnp.bfloat16), "dom", -offset).astype(
            jnp.float32
        )
        returned = lax.dynamic_update_index_in_dim(
            returned, arrived, (own_index + offset) % peers, 0
        )
    grad = grad.at[targets.reshape(-1)].add(
        (returned * live[:, :, None].astype(jnp.float32)).reshape(-1, width)
    )
    hub_back = lax.psum_scatter(hub_grad, "dom", scatter_dimension=0, tiled=True)
    grad = grad.at[hub_rows[0]].add(hub_back)
    return (out_rows, grad.astype(jnp.bfloat16), grad_self, grad_neigh)


def solution(mesh):
    return jax.shard_map(
        on_device,
        mesh=mesh,
        in_specs=(
            P("dom", None),
            P(),
            P(),
            P("dom", None),
            P("dom", None, None, None),
            P("dom", None, None),
            P("dom", None),
            P("dom", None),
            P("dom", None),
            P("dom", None),
        ),
        out_specs=(P("dom", None), P("dom", None), P(), P()),
        check_vma=False,
    )
```

profile of v0, /device:TPU:1, one launch (start us, length us, event | category | flops | bytes accessed | tf_op | source)
XLA Modules:
  0.0 314.4 jit_solution(17831394493580902880)
XLA Ops:
  9.0 6.8 %gather_fusion = bf16[1024,768]{1,0:T(8,128)(2,1)} fusion(bf16[512,768]{1,0:T(8,128)(2,1)} %param.10, s32[1024]{0:T(1024)S(1)} %broadcast_clamp_fusion), kind=kCustom, calls=%fused_computation | custom fusion | bytes 3149824 | tf_op jit(solution)/shard_map/gather | solution.py:39
  15.8 2.8 broadcast_multiply_fusion.1
  19.6 2.7 collective-permute-start
  26.6 3.7 %fusion.13 = f32[512,1024]{1,0:T(8,128)} fusion(bf16[512,768]{1,0:T(8,128)(2,1)S(1)} %copy-done.2, bf16[768,1024]{1,0:T(8,128)(2,1)} %param.11), kind=kOutput, calls=%fused_computation.77 | convolution fusion | flops 805306368 | bytes 4456448 | tf_op jit(solution)/shard_map/dot_general | solution.py:57
  31.0 40.9 %all-gather.1 = bf16[32,4,768]{2,1,0:T(4,128)(2,1)S(1)} all-gather(bf16[1,4,768]{2,1,0:T(4,128)(2,1)S(1)} %bitcast.137), channel_id=2, replica_groups=mesh['dom'=32] {'dom'}, dimensions={0}, use_global_device_ids=true | all-gather | bytes 202752 | tf_op jit(solution)/shard_map/all_gather | solution.py:46
  74.2 2.4 collective-permute-done.5
  79.9 4.5 %gather_fusion.2 = bf16[24,128,768]{2,1,0:T(8,128)(2,1)} fusion(bf16[7,128,768]{2,1,0:T(8,128)(2,1)} %bitcast.129, s32[1024]{0:T(1024)S(1)} %get-tuple-element.41), kind=kCustom, calls=%fused_computation.2 | custom fusion | bytes 9437280 | tf_op jit(solution)/shard_map/gather | solution.py:52
  84.4 3.8 %fusion = bf16[4,768,128]{1,2,0:T(8,128)(2,1)S(1)} fusion(bf16[4,6,128,768]{3,2,1,0:T(8,128)(2,1)} %bitcast.130, f32[4,128]{1,0:T(4,128)S(1)} %add_divide_fusion.1, s32[4,6,128,128]{3,2,1,0:T(8,128)} %param.14), kind=kOutput, calls=%fused_computation.12 | convolution fusion | flops 605159424 | bytes 7079936 | tf_op jit(solution)/shard_map/rkij,rkjf->rif/dot_general | solution.py:54
  88.2 2.7 multiply_convert_fusion
  93.1 2.7 convolution_bitcast_fusion.1
  95.8 2.7 fusion.15
  100.5 5.1 %convolution_bitcast_fusion = f32[4,6,128,768]{2,3,1,0:T(8,128)} fusion(f32[4,128,768]{1,2,0:T(8,128)S(1)} %copy.19, f32[4,128]{1,0:T(4,128)S(1)} %add_divide_fusion.1, s32[4,6,128,128]{3,2,1,0:T(8,128)S(1)} %copy-done.3), kind=kOutput, calls=%fused_computation.5 | convolution fusion | flops 605159424 | bytes 12584960 | tf_op jit(solution)/shard_map/rkij,rif->rkjf/dot_general | solution.py:73
  105.5 9.6 %copy.20 = f32[4,6,128,768]{3,2,1,0:T(8,128)} copy(f32[4,6,128,768]{2,3,1,0:T(8,128)} %convolution_bitcast_fusion) | data formatting | bytes 18874368 | tf_op jit(solution)/shard_map/rkij,rif->rkjf/dot_general | solution.py:73
  115.2 9.1 %copy.24 = f32[3,8,128,768]{3,1,2,0:T(8,128)S(1)} copy(f32[3,8,128,768]{3,2,1,0:T(8,128)} %bitcast.128) | data formatting | bytes 18874368
  124.3 3.5 %fusion.10 = f32[7,98304]{1,0:T(8,128)S(1)} fusion(f32[24,98304]{1,0:T(8,128)S(1)} %bitcast.127, s32[24]{0:T(128)S(1)} %eq.33), kind=kOutput, calls=%fused_computation.69 | convolution fusion | flops 198181024 | bytes 12189792 | tf_op jit(solution)/shard_map/dot_general | solution.py:78
  134.7 2.4 slice.49
  137.9 3.3 %convolution_add_fusion.1 = f32[512,768]{1,0:T(8,128)S(1)} fusion(f32[512,768]{1,0:T(8,128)} %slice.49, bf16[512,1024]{1,0:T(8,128)(2,1)S(1)} %copy-done.6, bf16[768,1024]{1,0:T(8,128)(2,1)} %param.11), kind=kOutput, calls=%fused_computation.15 | convolution fusion | flops 805699584 | bytes 5767168 | tf_op jit(solution)/shard_map/dot_general | solution.py:70
  141.2 5.1 %collective-permute-start.9 = (bf16[32,768]{1,0:T(8,128)(2,1)S(1)}, bf16[32,768]{1,0:T(8,128)(2,1)S(1)}, u32[]{:S(2)}, u32[]{:S(2)}) collective-permute-start(bf16[32,768]{1,0:T(8,128)(2,1)S(1)} %get-tuple-element.35), channel_id=1, source_target_pairs={{0,30},{1,31},{2,0},{3,1},{4,2},{5,3},{6,4},{7,5},{8,6},{9,7},{10,... | collective-permute-start | bytes 147464 | tf_op jit(solution)/shard_map/ppermute | solution.py:11
  152.5 3.9 %collective-permute-done.13 = bf16[32,768]{1,0:T(8,128)(2,1)S(1)} collective-permute-done((bf16[32,768]{1,0:T(8,128)(2,1)S(1)}, bf16[32,768]{1,0:T(8,128)(2,1)S(1)}, u32[]{:S(2)}, u32[]{:S(2)}) %collective-permute-start.13) | collective-permute-done | bytes 49184 | tf_op jit(solution)/shard_map/ppermute | solution.py:11
  156.5 2.8 collective-permute-done.14
  161.6 8.6 %scatter_fusion = f32[512,768]{1,0:T(8,128)S(1)} fusion(f32[512,768]{1,0:T(8,128)S(1)} %convolution_add_fusion.1, s32[1024]{0:T(1024)S(1)} %bitcast.138, f32[1024,768]{1,0:T(8,128)} %bitcast.131), kind=kCustom, calls=%fused_computation.3 | custom fusion | flops 786432 | bytes 9441280 | tf_op jit(solution)/shard_map/scatter-add | solution.py:96
  170.2 127.3 %all-reduce.4.cloned.1.call-done = (f32[128,768]{1,0:T(8,128)}, f32[768,1024]{0,1:T(8,128)}, f32[768,1024]{1,0:T(8,128)}) async-done(((f32[128,768]{1,0:T(8,128)}, f32[768,1024]{0,1:T(8,128)}, f32[768,1024]{1,0:T(8,128)}), (f32[128,768]{1,0:T(8,128)}, f32[768,1024]{0,1:T(8,128)}, f32[768,1024]{1,0:T(8,128)})) %all-reduce.4.cloned.1.call-update) | async-done | bytes 6684688
  299.9 3.5 %copy.21 = f32[768,1024]{1,0:T(8,128)} copy(f32[768,1024]{0,1:T(8,128)} %get-tuple-element.17) | data formatting | bytes 6291456
  303.5 4.1 %copy.45 = f32[768,1024]{1,0:T(8,128)} copy(f32[768,1024]{1,0:T(8,128)} %get-tuple-element.46) | data formatting | bytes 6291456
  (104 shorter events, 35.8 us)
Async XLA Ops:
  7.2 81.0 %copy-start = (bf16[768,1024]{1,0:T(8,128)(2,1)S(1)}, bf16[768,1024]{1,0:T(8,128)(2,1)}, u32[]{:S(2)}) copy-start(bf16[768,1024]{1,0:T(8,128)(2,1)} %param.12) | copy-start | bytes 4718596
  7.2 290.4 %all-reduce.4.cloned.1.call-start = ((), (), s32[]{:S(2)}) async-start(), calls=%async_computation | async-start | bytes 13369344
  15.8 10.8 %copy-start.2 = (bf16[512,768]{1,0:T(8,128)(2,1)S(1)}, bf16[512,768]{1,0:T(8,128)(2,1)}, u32[]{:S(2)}) copy-start(bf16[512,768]{1,0:T(8,128)(2,1)} %param.10) | copy-start | bytes 2359300
  19.6 54.1 %collective-permute-start = (bf16[32,768]{1,0:T(8,128)(2,1)S(1)}, bf16[32,768]{1,0:T(8,128)(2,1)S(1)}, u32[]{:S(2)}, u32[]{:S(2)}) collective-permute-start(bf16[32,768]{1,0:T(8,128)(2,1)S(1)} %get-tuple-element.28), channel_id=1, source_target_pairs={{0,1},{1,2},{2,3},{3,4},{4,5},{5,6},{6,7},{7,8},{8,9},{9,10},{10,1... | collective-permute-start | bytes 147464 | tf_op jit(solution)/shard_map/ppermute | solution.py:11
  22.3 51.7 %collective-permute-start.1 = (bf16[32,768]{1,0:T(8,128)(2,1)S(1)}, bf16[32,768]{1,0:T(8,128)(2,1)S(1)}, u32[]{:S(2)}, u32[]{:S(2)}) collective-permute-start(bf16[32,768]{1,0:T(8,128)(2,1)S(1)} %get-tuple-element.27), channel_id=1, source_target_pairs={{0,2},{1,3},{2,4},{3,5},{4,6},{5,7},{6,8},{7,9},{8,10},{9,11},{10,... | collective-permute-start | bytes 147464 | tf_op jit(solution)/shard_map/ppermute | solution.py:11
  23.5 50.6 %collective-permute-start.2 = (bf16[32,768]{1,0:T(8,128)(2,1)S(1)}, bf16[32,768]{1,0:T(8,128)(2,1)S(1)}, u32[]{:S(2)}, u32[]{:S(2)}) collective-permute-start(bf16[32,768]{1,0:T(8,128)(2,1)S(1)} %get-tuple-element.26), channel_id=1, source_target_pairs={{0,3},{1,4},{2,5},{3,6},{4,7},{5,8},{6,9},{7,10},{8,11},{9,12},{10... | collective-permute-start | bytes 147464 | tf_op jit(solution)/shard_map/ppermute | solution.py:11
  23.8 50.3 %collective-permute-start.3 = (bf16[32,768]{1,0:T(8,128)(2,1)S(1)}, bf16[32,768]{1,0:T(8,128)(2,1)S(1)}, u32[]{:S(2)}, u32[]{:S(2)}) collective-permute-start(bf16[32,768]{1,0:T(8,128)(2,1)S(1)} %get-tuple-element.25), channel_id=1, source_target_pairs={{0,4},{1,5},{2,6},{3,7},{4,8},{5,9},{6,10},{7,11},{8,12},{9,13},{1... | collective-permute-start | bytes 147464 | tf_op jit(solution)/shard_map/ppermute | solution.py:11
  25.1 5.2 %copy-start.8 = (s32[4,6]{1,0:T(4,128)S(1)}, s32[4,6]{1,0:T(4,128)}, u32[]{:S(2)}) copy-start(s32[4,6]{1,0:T(4,128)} %param.13) | copy-start | bytes 292
  25.1 5.3 %copy-start.10 = (s32[1,4]{1,0:T(1,128)S(1)}, s32[1,4]{1,0:T(1,128)}, u32[]{:S(2)}) copy-start(s32[1,4]{1,0:T(1,128)} %param.17) | copy-start | bytes 52
  25.1 46.9 %copy-start.11 = (s32[1,128]{1,0:T(1,128)S(1)}, s32[1,128]{1,0:T(1,128)}, u32[]{:S(2)}) copy-start(s32[1,128]{1,0:T(1,128)} %param.18) | copy-start | bytes 1540
  25.1 49.1 %collective-permute-start.4 = (bf16[32,768]{1,0:T(8,128)(2,1)S(1)}, bf16[32,768]{1,0:T(8,128)(2,1)S(1)}, u32[]{:S(2)}, u32[]{:S(2)}) collective-permute-start(bf16[32,768]{1,0:T(8,128)(2,1)S(1)} %get-tuple-element.24), channel_id=1, source_target_pairs={{0,31},{1,0},{2,1},{3,2},{4,3},{5,4},{6,5},{7,6},{8,7},{9,8},{10,9... | collective-permute-start | bytes 147464 | tf_op jit(solution)/shard_map/ppermute | solution.py:11
  73.7 2.9 collective-permute-start.5
  74.0 3.9 %collective-permute-start.6 = (bf16[32,768]{1,0:T(8,128)(2,1)S(1)}, bf16[32,768]{1,0:T(8,128)(2,1)S(1)}, u32[]{:S(2)}, u32[]{:S(2)}) collective-permute-start(bf16[32,768]{1,0:T(8,128)(2,1)S(1)} %get-tuple-element.22), channel_id=1, source_target_pairs={{0,29},{1,30},{2,31},{3,0},{4,1},{5,2},{6,3},{7,4},{8,5},{9,6},{10... | collective-permute-start | bytes 147464 | tf_op jit(solution)/shard_map/ppermute | solution.py:11
  74.1 4.6 %collective-permute-start.7 = (bf16[32,768]{1,0:T(8,128)(2,1)S(1)}, bf16[32,768]{1,0:T(8,128)(2,1)S(1)}, u32[]{:S(2)}, u32[]{:S(2)}) collective-permute-start(bf16[32,768]{1,0:T(8,128)(2,1)S(1)} %get-tuple-element.21), channel_id=1, source_target_pairs={{0,28},{1,29},{2,30},{3,31},{4,0},{5,1},{6,2},{7,3},{8,4},{9,5},{1... | collective-permute-start | bytes 147464 | tf_op jit(solution)/shard_map/ppermute | solution.py:11
  90.9 4.9 %copy-start.5 = (bf16[512,1024]{1,0:T(8,128)(2,1)}, bf16[512,1024]{1,0:T(8,128)(2,1)S(1)}, u32[]{:S(2)}) copy-start(bf16[512,1024]{1,0:T(8,128)(2,1)S(1)} %get-tuple-element.19) | copy-start | bytes 3145732
  137.5 10.1 %collective-permute-start.8 = (bf16[32,768]{1,0:T(8,128)(2,1)S(1)}, bf16[32,768]{1,0:T(8,128)(2,1)S(1)}, u32[]{:S(2)}, u32[]{:S(2)}) collective-permute-start(bf16[32,768]{1,0:T(8,128)(2,1)S(1)} %get-tuple-element.36), channel_id=1, source_target_pairs={{0,31},{1,0},{2,1},{3,2},{4,3},{5,4},{6,5},{7,6},{8,7},{9,8},{10,9... | collective-permute-start | bytes 147464 | tf_op jit(solution)/shard_map/ppermute | solution.py:11
  141.2 8.8 %collective-permute-start.9 = (bf16[32,768]{1,0:T(8,128)(2,1)S(1)}, bf16[32,768]{1,0:T(8,128)(2,1)S(1)}, u32[]{:S(2)}, u32[]{:S(2)}) collective-permute-start(bf16[32,768]{1,0:T(8,128)(2,1)S(1)} %get-tuple-element.35), channel_id=1, source_target_pairs={{0,30},{1,31},{2,0},{3,1},{4,2},{5,3},{6,4},{7,5},{8,6},{9,7},{10,... | collective-permute-start | bytes 147464 | tf_op jit(solution)/shard_map/ppermute | solution.py:11
  146.3 4.8 %collective-permute-start.10 = (bf16[32,768]{1,0:T(8,128)(2,1)S(1)}, bf16[32,768]{1,0:T(8,128)(2,1)S(1)}, u32[]{:S(2)}, u32[]{:S(2)}) collective-permute-start(bf16[32,768]{1,0:T(8,128)(2,1)S(1)} %get-tuple-element.34), channel_id=1, source_target_pairs={{0,29},{1,30},{2,31},{3,0},{4,1},{5,2},{6,3},{7,4},{8,5},{9,6},{10... | collective-permute-start | bytes 147464 | tf_op jit(solution)/shard_map/ppermute | solution.py:11
  147.0 5.5 %collective-permute-start.11 = (bf16[32,768]{1,0:T(8,128)(2,1)S(1)}, bf16[32,768]{1,0:T(8,128)(2,1)S(1)}, u32[]{:S(2)}, u32[]{:S(2)}) collective-permute-start(bf16[32,768]{1,0:T(8,128)(2,1)S(1)} %get-tuple-element.33), channel_id=1, source_target_pairs={{0,28},{1,29},{2,30},{3,31},{4,0},{5,1},{6,2},{7,3},{8,4},{9,5},{1... | collective-permute-start | bytes 147464 | tf_op jit(solution)/shard_map/ppermute | solution.py:11
  147.0 5.5 %collective-permute-start.12 = (bf16[32,768]{1,0:T(8,128)(2,1)S(1)}, bf16[32,768]{1,0:T(8,128)(2,1)S(1)}, u32[]{:S(2)}, u32[]{:S(2)}) collective-permute-start(bf16[32,768]{1,0:T(8,128)(2,1)S(1)} %get-tuple-element.32), channel_id=1, source_target_pairs={{0,1},{1,2},{2,3},{3,4},{4,5},{5,6},{6,7},{7,8},{8,9},{9,10},{10,1... | collective-permute-start | bytes 147464 | tf_op jit(solution)/shard_map/ppermute | solution.py:11
  147.5 8.9 %collective-permute-start.13 = (bf16[32,768]{1,0:T(8,128)(2,1)S(1)}, bf16[32,768]{1,0:T(8,128)(2,1)S(1)}, u32[]{:S(2)}, u32[]{:S(2)}) collective-permute-start(bf16[32,768]{1,0:T(8,128)(2,1)S(1)} %get-tuple-element.31), channel_id=1, source_target_pairs={{0,2},{1,3},{2,4},{3,5},{4,6},{5,7},{6,8},{7,9},{8,10},{9,11},{10,... | collective-permute-start | bytes 147464 | tf_op jit(solution)/shard_map/ppermute | solution.py:11
  150.0 9.3 %collective-permute-start.14 = (bf16[32,768]{1,0:T(8,128)(2,1)S(1)}, bf16[32,768]{1,0:T(8,128)(2,1)S(1)}, u32[]{:S(2)}, u32[]{:S(2)}) collective-permute-start(bf16[32,768]{1,0:T(8,128)(2,1)S(1)} %get-tuple-element.30), channel_id=1, source_target_pairs={{0,3},{1,4},{2,5},{3,6},{4,7},{5,8},{6,9},{7,10},{8,11},{9,12},{10... | collective-permute-start | bytes 147464 | tf_op jit(solution)/shard_map/ppermute | solution.py:11
  151.1 8.5 %collective-permute-start.15 = (bf16[32,768]{1,0:T(8,128)(2,1)S(1)}, bf16[32,768]{1,0:T(8,128)(2,1)S(1)}, u32[]{:S(2)}, u32[]{:S(2)}) collective-permute-start(bf16[32,768]{1,0:T(8,128)(2,1)S(1)} %get-tuple-element.29), channel_id=1, source_target_pairs={{0,4},{1,5},{2,6},{3,7},{4,8},{5,9},{6,10},{7,11},{8,12},{9,13},{1... | collective-permute-start | bytes 147464 | tf_op jit(solution)/shard_map/ppermute | solution.py:11
  303.5 4.1 %copy-start.1 = (bf16[768,1024]{1,0:T(8,128)(2,1)S(1)}, bf16[768,1024]{1,0:T(8,128)(2,1)}, u32[]{:S(2)}) copy-start(bf16[768,1024]{1,0:T(8,128)(2,1)} %param.12) | copy-start | bytes 4718596
  (7 other events, 17.7 us)
Sparse Core Ops, SparseCore 0:
  131.7 165.8 all-reduce.3
where the time goes:
time: 316 us; the launch traced here: 314 us
  waiting for transfers between devices  139 us (44%)
  local copies, waits for them, and re-layouts  50.7 us (16%)
  blocking collectives  40.9 us (13%)
  matrix products  29.6 us (9%)
  other arithmetic  21.1 us (7%)
  starting transfers between devices  18.4 us (6%)
  between operations  14.5 us (5%)
    unnamed x2, waiting for transfers between devices  127 us
    all_gather x1, blocking collectives, on_device(): all_hubs = lax.all_gather(own_hubs, 'dom', axis=0, tiled=True)  40.9 us
    unnamed x37, local copies, waits for them, and re-layouts  19.3 us
    ppermute x16, starting transfers between devices, shifted(): lax.ppermute(array, axis, [(i, (i + by) % length) for i in range(length)])  18.3 us
    ppermute x16, waiting for transfers between devices, shifted(): lax.ppermute(array, axis, [(i, (i + by) % length) for i in range(length)])  12 us
    dot_general x1, local copies, waits for them, and re-layouts, on_device(): jnp.einsum('rkij,rif->rkjf', weights, scaled, preferred_element_type=jnp....  9.62 us
    scatter-add x1, other arithmetic, on_device(): grad.at[targets.reshape(-1)]  8.58 us
    gather x1, local copies, waits for them, and re-layouts, on_device(): outgoing = features[targets] * live[:, :, None].astype(jnp.bfloat16)  6.8 us
  transfers between devices with their start and end apart: 17, of which 8 were waited for; matrix products, arithmetic and copies ran while one was open for 8% of the time, Pallas kernels for 0%

commit v1 on v0

v1 whole, which is shorter than its diff:
```python
import functools

import jax
import jax.numpy as jnp
from jax import lax
from jax.experimental import pallas as pl
from jax.experimental.pallas import tpu as pltpu
from jax.sharding import PartitionSpec as P

REACH = 4
MESH = pl.DeviceIdType.MESH
F32 = jnp.float32
BF16 = jnp.bfloat16
GROUPS = 3


def near_offsets(reach):
    return list(range(1, reach + 1)) + [-distance for distance in range(1, reach + 1)]


def bit_orders(peers):
    bits = list(range(1, peers.bit_length() - 1))
    head, tail = bits[:-1], bits[-1:]
    orders = []
    for group in range(GROUPS):
        turn = group * len(head) // GROUPS
        orders.append(head[turn:] + head[:turn] + tail)
    return orders


def halves(rows, cols, steps):
    sizes = [(rows, cols)]
    for _ in range(steps):
        rows, cols = (rows // 2, cols) if rows > 16 else (rows, cols // 2)
        sizes.append((rows, cols))
    return sizes


def dot(left, right, dims=((1,), (0,))):
    return lax.dot_general(left, right, (dims, ((), ())), preferred_element_type=F32)


def layer(peers, offsets, sizes, cols_ref, feat_ref, ws_ref, wn_ref, tiles_ref, pick_ref, flag_ref, cot_ref,
          out_ref, gfeat_ref, res_ref, *scratch):
    steps = len(sizes) - 1
    (x, adj, inv, scat, going, halo, hub_out, hub_in, hub_all, pre, dpre, dneigh, own, back_out, back,
     hback_out, hback, core_out, core_in, acc) = scratch[:20]
    rs_out, rs_in = scratch[20:20 + steps], scratch[20 + steps:20 + 2 * steps]
    (halo_s, halo_r, hub_s, hub_r, back_s, back_r, hback_s, hback_r, core_s, core_r, rs_s, rs_r,
     ag_s, ag_r, last_s, last_r) = scratch[20 + 2 * steps:]
    me = lax.axis_index("dom")
    core = me % 2
    mate = me + 1 - 2 * core
    rows, width = feat_ref.shape
    hid = ws_ref.shape[1]
    row_blocks, slots, tile, _ = tiles_ref.shape
    col_blocks = adj.shape[1] // tile
    caps = halo.shape[0]
    orders = bit_orders(peers)
    grows = width // GROUPS

    def remote(src, dst, send, recv, peer):
        return pltpu.make_async_remote_copy(
            src_ref=src, dst_ref=dst, send_sem=send, recv_sem=recv, device_id=(peer,), device_id_type=MESH
        )

    barrier = pltpu.get_barrier_semaphore()

    def greet(k, carry):
        pl.semaphore_signal(barrier, inc=1, device_id=(lax.rem(me + k, peers),), device_id_type=MESH)
        return carry

    lax.fori_loop(1, peers, greet, 0)

    picks = pick_ref.shape[1]
    scat[...] = (lax.broadcasted_iota(jnp.int32, (rows, picks), 0) == pick_ref[...]).astype(F32).astype(BF16)
    x[0] = feat_ref[...]
    picked = dot(scat[...], feat_ref[...], ((0,), (0,)))
    going[...] = picked[:caps].astype(BF16)
    hub_out[...] = picked[caps:caps + 4]
    hub_in[me] = picked[caps:caps + 4]
    pl.semaphore_wait(barrier, peers - 1)

    part = caps // len(offsets)

    def halo_copy(q):
        piece = pl.ds(q * part, part)
        return remote(going.at[piece], halo.at[piece], halo_s.at[q], halo_r.at[q],
                      lax.rem(me + offsets[q] + peers, peers))

    def hub_copy(k):
        return remote(hub_out, hub_in.at[me], hub_s.at[k], hub_r.at[k], lax.rem(me + k, peers))

    def back_copy(q):
        piece = pl.ds(q * part, part)
        return remote(back_out.at[piece], back.at[piece], back_s.at[q], back_r.at[q],
                      lax.rem(me - offsets[q] + peers, peers))

    def hback_copy(k):
        peer = lax.rem(me + k, peers)
        return remote(hback_out.at[peer], hback.at[me], hback_s.at[k], hback_r.at[k], peer)

    def start_all(make):
        def body(k, carry):
            make(k).start()
            return carry
        lax.fori_loop(1, peers, body, 0)

    def wait_recv_all(make):
        def body(k, carry):
            make(k).wait_recv()
            return carry
        lax.fori_loop(1, peers, body, 0)

    def wait_send_all(make):
        def body(k, carry):
            make(k).wait_send()
            return carry
        lax.fori_loop(1, peers, body, 0)

    start_all(hub_copy)
    for q in range(len(offsets)):
        halo_copy(q).start()

    def build(b, carry):
        weights = [tiles_ref[b, k].astype(F32) for k in range(slots)]
        at = pl.ds(pl.multiple_of(b * tile, tile), tile)
        inv[at, :] = 1.0 / (jnp.sum(sum(weights), axis=1, keepdims=True) + 1.0)
        for t in range(col_blocks):
            total = jnp.zeros((tile, tile), F32)
            for k in range(slots):
                total = total + weights[k] * (cols_ref[b, k] == t).astype(F32)
            if t * tile >= rows + caps:
                first = t * tile - rows - caps
                total = total * flag_ref[:, first:first + tile].astype(F32)
            adj[at, t * tile:(t + 1) * tile] = total.astype(BF16)
        return carry

    lax.fori_loop(0, row_blocks, build, 0)
    half = rows // 2
    for r in range(2):
        at = slice(r * half, (r + 1) * half)
        own[at] = dot(adj[at, :rows], feat_ref[...])
        pre[at] = dot(feat_ref[at], ws_ref[...])

    for q in range(len(offsets)):
        halo_copy(q).wait_recv()
    wait_recv_all(hub_copy)
    for j in range(0, peers, 4):
        hub_all[4 * j:4 * j + 16] = jnp.concatenate([hub_in[j + i] for i in range(4)], axis=0).astype(BF16)

    for r in range(2):
        at = slice(r * half, (r + 1) * half)
        total = own[at] + dot(adj[at, rows:rows + caps], halo[...]) + dot(adj[at, rows + caps:], hub_all[...])
        neigh = (total * inv[at]).astype(BF16)
        x[1, at] = neigh
        whole = pre[at] + dot(neigh, wn_ref[...])
        sigma = jax.nn.sigmoid(whole)
        out_ref[at] = (whole * sigma).astype(BF16)
        dpre[at] = (cot_ref[at].astype(F32) * sigma * (1.0 + whole * (1.0 - sigma))).astype(BF16)

    def core_copy(g):
        return remote(core_out.at[g], core_in.at[g], core_s.at[g], core_r.at[g], mate)

    for g in range(GROUPS):
        core_out[g] = dot(x[1 - core, :, g * grows:(g + 1) * grows], dpre[...], ((0,), (0,))).astype(BF16)
        core_copy(g).start()
    for g in range(GROUPS):
        acc[g] = dot(x[core, :, g * grows:(g + 1) * grows], dpre[...], ((0,), (0,)))

    zero = me * 0
    places = [(zero, zero)] * GROUPS
    trail = [[None] * steps for _ in range(GROUPS)]

    def ds(row, col, size):
        unit = min(size[0], grows)
        return (pl.ds(pl.multiple_of(row, 16), unit), pl.ds(pl.multiple_of(col, 128), size[1]))

    def rs_copy(s, g):
        step = 2 ** orders[g][s]
        bit = (me // step) % 2
        return remote(rs_out[s].at[g], rs_in[s].at[g], rs_s.at[s, g], rs_r.at[s, g], me + step - 2 * step * bit)

    def rs_start(s, g):
        row, col = places[g]
        size = sizes[s + 1]
        bit = (me // 2 ** orders[g][s]) % 2
        if size[0] != sizes[s][0]:
            keep, give = (row + bit * size[0], col), (row + (1 - bit) * size[0], col)
        else:
            keep, give = (row, col + bit * size[1]), (row, col + (1 - bit) * size[1])
        rs_out[s][g] = acc[(g, *ds(*give, size))].astype(BF16)
        rs_copy(s, g).start()
        places[g] = keep

    def rs_end(s, g):
        rs_copy(s, g).wait_recv()
        spot = (g, *ds(*places[g], sizes[s + 1]))
        acc[spot] = acc[spot] + rs_in[s][g].astype(F32)

    def ag_place(s, g):
        row, col = zero, zero
        for t in range(s + 1):
            bit = (me // 2 ** orders[g][t]) % 2
            if sizes[t + 1][0] != sizes[t][0]:
                row = row + bit * sizes[t + 1][0]
            else:
                col = col + bit * sizes[t + 1][1]
        return row, col

    def ag_copy(s, g):
        step = 2 ** orders[g][s]
        bit = (me // step) % 2
        row, col = ag_place(s, g)
        size = sizes[s + 1]
        spot = res_ref.at[(core, *ds(row + g * grows, col, size))]
        return remote(spot, spot, ag_s.at[s, g], ag_r.at[s, g], me + step - 2 * step * bit)

    def last_copy(g):
        spot = res_ref.at[core, pl.ds(g * grows, grows)]
        return remote(spot, spot, last_s.at[g], last_r.at[g], mate)

    for g in range(GROUPS):
        core_copy(g).wait_recv()
        acc[g] = acc[g] + core_in[g].astype(F32)
        rs_start(0, g)

    for r in range(2):
        at = slice(r * half, (r + 1) * half)
        dneigh[at] = (dot(dpre[at], wn_ref[...], ((1,), (1,))) * inv[at]).astype(BF16)
    back_out[...] = dot(adj[:, rows:rows + caps], dneigh[...], ((0,), (0,))).astype(BF16)
    hubs = dot(adj[:, rows + caps:], dneigh[...], ((0,), (0,)))
    for j in range(peers):
        hback_out[j] = hubs[4 * j:4 * j + 4]
    hback[me] = hback_out[me]
    for q in range(len(offsets)):
        back_copy(q).start()
    start_all(hback_copy)

    for s in range(steps):
        for g in range(GROUPS):
            rs_end(s, g)
            if s + 1 < steps:
                rs_start(s + 1, g)
            else:
                spot = ds(places[g][0] + g * grows, places[g][1], sizes[steps])
                res_ref[(core, *spot)] = acc[(g, *ds(*places[g], sizes[steps]))].astype(BF16)
                ag_copy(steps - 1, g).start()
        if s == 0:
            for r in range(2):
                at = slice(r * half, (r + 1) * half)
                own[at] = dot(dpre[at], ws_ref[...], ((1,), (1,)))
            own[...] += dot(adj[:, :rows], dneigh[...], ((0,), (0,)))

    for s in reversed(range(steps)):
        for g in range(GROUPS):
            ag_copy(s, g).wait_recv()
            if s > 0:
                ag_copy(s - 1, g).start()
            else:
                last_copy(g).start()

    for q in range(len(offsets)):
        back_copy(q).wait_recv()
    wait_recv_all(hback_copy)
    hub_sum = jnp.sum(hback[...], axis=0)
    coarse = hub_sum.astype(BF16).astype(F32)
    hub_part = jnp.concatenate(
        [coarse, hub_sum - coarse, jnp.zeros((picks - caps - 8, width), F32)], axis=0
    ).astype(BF16)
    for r in range(2):
        at = slice(r * half, (r + 1) * half)
        total = own[at] + dot(scat[at, :caps], back[...]) + dot(scat[at, caps:], hub_part)
        gfeat_ref[at] = total.astype(BF16)

    for g in range(GROUPS):
        last_copy(g).wait_recv()
    for q in range(len(offsets)):
        halo_copy(q).wait_send()
        back_copy(q).wait_send()
    wait_send_all(hub_copy)
    wait_send_all(hback_copy)
    for g in range(GROUPS):
        core_copy(g).wait_send()
        last_copy(g).wait_send()
        for s in range(steps):
            rs_copy(s, g).wait_send()
            ag_copy(s, g).wait_send()


def on_device(peers, features, w_self, w_neigh, tile_cols, tile_weights, send_rows, send_counts, hub_rows, readers,
              cotangent):
    me = lax.axis_index("dom")
    rows, width = features.shape
    hid = w_self.shape[1]
    cap = send_rows.shape[2]
    offsets = near_offsets(REACH)
    caps = len(offsets) * cap
    hubs = readers.shape[1]
    tile = tile_weights.shape[2]
    targets = jnp.where(
        jnp.arange(cap, dtype=jnp.int32)[None, :] < send_counts[0][:, None], send_rows[0], -1
    )
    wrapped = jnp.concatenate([targets[-REACH:], targets, targets[:REACH]], axis=0)
    window = lax.dynamic_slice_in_dim(wrapped, me, 2 * REACH + 1, 0)
    lists = [window[REACH + offset] for offset in offsets]
    spare = jnp.full((tile - 2 * hub_rows.shape[1],), -1, jnp.int32)
    pick = jnp.concatenate(lists + [hub_rows[0], hub_rows[0], spare])[None, :]
    picks = pick.shape[1]

    steps = peers.bit_length() - 2
    grows = width // GROUPS
    sizes = halves(grows, hid, steps)
    dma = pltpu.SemaphoreType.DMA
    vmem = pltpu.VMEM
    scratch = [
        vmem((2, rows, width), BF16),
        vmem((rows, rows + caps + hubs), BF16),
        vmem((rows, 1), F32),
        vmem((rows, picks), BF16),
        vmem((caps, width), BF16),
        vmem((caps, width), BF16),
        vmem((4, width), F32),
        vmem((peers, 4, width), F32),
        vmem((hubs, width), BF16),
        vmem((rows, hid), F32),
        vmem((rows, hid), BF16),
        vmem((rows, width), BF16),
        vmem((rows, width), F32),
        vmem((caps, width), BF16),
        vmem((caps, width), BF16),
        vmem((peers, 4, width), F32),
        vmem((peers, 4, width), F32),
        vmem((GROUPS, grows, hid), BF16),
        vmem((GROUPS, grows, hid), BF16),
        vmem((GROUPS, grows, hid), F32),
    ]
    scratch += [vmem((GROUPS, *sizes[s + 1]), BF16) for s in range(steps)] * 2
    q = len(offsets)
    scratch += [
        dma((q,)), dma((q,)), dma((peers,)), dma((peers,)), dma((q,)), dma((q,)), dma((peers,)), dma((peers,)),
        dma((GROUPS,)), dma((GROUPS,)), dma((steps, GROUPS)), dma((steps, GROUPS)),
        dma((steps, GROUPS)), dma((steps, GROUPS)), dma((GROUPS,)), dma((GROUPS,)),
    ]
    whole = pl.BlockSpec(memory_space=pltpu.VMEM)
    out_rows, grad, both = pl.pallas_call(
        functools.partial(layer, peers, offsets, sizes),
        out_shape=(
            jax.ShapeDtypeStruct((rows, hid), BF16),
            jax.ShapeDtypeStruct((rows, width), BF16),
            jax.ShapeDtypeStruct((2, width, hid), BF16),
        ),
        in_specs=[pl.BlockSpec(memory_space=pltpu.SMEM)] + [whole] * 7,
        out_specs=(whole,) * 3,
        scratch_shapes=scratch,
        compiler_params=pltpu.CompilerParams(
            collective_id=0, has_side_effects=True, vmem_limit_bytes=56 * 1024 * 1024
        ),
        cost_estimate=pl.CostEstimate(
            flops=8 * 2 * rows * width * hid, bytes_accessed=16 * rows * width * 2, transcendentals=rows * hid
        ),
    )(tile_cols, features, w_self, w_neigh, tile_weights, pick, readers, cotangent)
    return out_rows, grad, both[0].astype(F32), both[1].astype(F32)


def solution(mesh):
    peers = mesh.shape["dom"]
    return jax.shard_map(
        functools.partial(on_device, peers),
        mesh=mesh,
        in_specs=(
            P("dom", None),
            P(),
            P(),
            P("dom", None),
            P("dom", None, None, None),
            P("dom", None, None),
            P("dom", None),
            P("dom", None),
            P("dom", None),
            P("dom", None),
        ),
        out_specs=(P("dom", None), P("dom", None), P(), P()),
        check_vma=False,
    )
```

time: 316 us -> 94 us (0.30)
  waiting for transfers between devices: 139 us -> 0 us
  Pallas kernels: 0 us -> 83.5 us
  local copies, waits for them, and re-layouts: 50.7 us -> 3.26 us
  blocking collectives: 40.9 us -> 0 us
  matrix products: 29.6 us -> 0 us
  starting transfers between devices: 18.4 us -> 0 us
  other arithmetic: 21.1 us -> 6.27 us
  between operations: 14.5 us -> 0.68 us
    unnamed x2 -> x0, waiting for transfers between devices: 127 us -> none
    pallas_call x0 -> x1, Pallas kernels: none -> 83.5 us  [on_device(): pl.pallas_call(functools.partial(layer, peers, offsets, sizes), out_shape...]
    all_gather x1 -> x0, blocking collectives: 40.9 us -> none  [on_device(): all_hubs = lax.all_gather(own_hubs, 'dom', axis=0, tiled=True)]
    dot_general x9 -> x0, matrix products: 29.6 us -> none  [the longest x1 5.05 us: on_device(): jnp.einsum('rkij,rif->rkjf', weights, scaled, preferred_element_type=jnp....]
    ppermute x16 -> x0, starting transfers between devices: 18.3 us -> none  [shifted(): lax.ppermute(array, axis, [(i, (i + by) % length) for i in range(length)])]
    unnamed x37 -> x6, local copies, waits for them, and re-layouts: 19.3 us -> 1.86 us
    ppermute x16 -> x0, waiting for transfers between devices: 12 us -> none  [shifted(): lax.ppermute(array, axis, [(i, (i + by) % length) for i in range(length)])]
    gather x3 -> x0, local copies, waits for them, and re-layouts: 11.8 us -> none  [the longest x1 6.8 us: on_device(): outgoing = features[targets] * live[:, :, None].astype(jnp.bfloat16)]
  transfers between devices with their start and end apart: 17 -> 0, of which waited for: 8 -> 0; matrix products, arithmetic and copies ran while one was open for 8% -> 0% of each run, Pallas kernels for 0% -> 0%
where the time goes in v1:
time: 94 us; the launch traced here: 93.7 us
  Pallas kernels  83.5 us (89%)
  other arithmetic  6.27 us (7%)
  local copies, waits for them, and re-layouts  3.26 us (3%)
    pallas_call x1, Pallas kernels, on_device(): pl.pallas_call(functools.partial(layer, peers, offsets, sizes), out_shape...  83.5 us
    convert_element_type x1, other arithmetic, on_device(): return (out_rows, grad, both[0].astype(F32), both[1].astype(F32))  5.46 us

profile of v1, /device:TPU:1, one launch (start us, length us, event | category | flops | bytes accessed | tf_op | source)
XLA Modules:
  0.0 93.7 jit_solution(6686894871278627022)
XLA Ops:
  0.6 0.8 bitcast_select_fusion
  1.5 0.8 concatenate.7
  2.3 0.6 broadcast_in_dim.13.pick_ref
  2.9 83.5 %shard_map.129 = (bf16[512,1024]{1,0:T(8,128)(2,1)}, bf16[512,768]{1,0:T(8,128)(2,1)}, bf16[2,768,1024]{2,1,0:T(8,128)(2,1)}) custom-call(s32[4,6]{1,0:T(4,128)} %cols_ref.1, bf16[512,768]{1,0:T(8,128)(2,1)} %feat_ref.1, bf16[768,1024]{1,0:T(8,128)(2,1)} %ws_ref.1, bf16[768,1024]{1,0:T(8,128)(2,1)} %wn_ref.1, s32[4,6,128,128]{3,2,1,0:T(8,128)} %tiles_ref.1, ...), custom_call_target="tpu_custom_call" | custom-call | flops 6442450944 | bytes 12582912 | tf_op jit(solution)/shard_map/pallas_call | solution.py:346
  86.4 0.0 copy-start
  86.4 0.0 copy-start.1
  86.4 5.5 %bitcast_convert_fusion = (f32[768,1024]{1,0:T(8,128)}, f32[768,1024]{1,0:T(8,128)}) fusion(bf16[2,768,1024]{2,1,0:T(8,128)(2,1)} %get-tuple-element.9), kind=kLoop, calls=%fused_computation | loop fusion | flops 1572864 | bytes 9437184 | tf_op jit(solution)/shard_map/convert_element_type | solution.py:363
  91.9 0.0 copy-done
  91.9 1.0 %copy.16 = bf16[512,1024]{1,0:T(8,128)(2,1)} copy(bf16[512,1024]{1,0:T(8,128)(2,1)S(1)} %copy-done) | data formatting | bytes 2097152
  92.9 0.0 copy-done.1
  92.9 0.9 copy.17
  (4 shorter events, 0.0 us)
Async XLA Ops:
  86.4 5.5 %copy-start = (bf16[512,1024]{1,0:T(8,128)(2,1)S(1)}, bf16[512,1024]{1,0:T(8,128)(2,1)}, u32[]{:S(2)}) copy-start(bf16[512,1024]{1,0:T(8,128)(2,1)} %get-tuple-element.26) | copy-start | bytes 3145732
  86.4 6.4 %copy-start.1 = (bf16[512,768]{1,0:T(8,128)(2,1)S(1)}, bf16[512,768]{1,0:T(8,128)(2,1)}, u32[]{:S(2)}) copy-start(bf16[512,768]{1,0:T(8,128)(2,1)} %get-tuple-element.27) | copy-start | bytes 2359300

commit v2 on v1

--- a/solution.py
+++ b/solution.py
@@ -11,7 +11,8 @@
 MESH = pl.DeviceIdType.MESH
 F32 = jnp.float32
 BF16 = jnp.bfloat16
-GROUPS = 3
+GROUPS = 6
+QUAD = 4
 
 
 def near_offsets(reach):
@@ -23,8 +24,11 @@
     head, tail = bits[:-1], bits[-1:]
     orders = []
     for group in range(GROUPS):
-        turn = group * len(head) // GROUPS
-        orders.append(head[turn:] + head[:turn] + tail)
+        turn = (group % 3) * len(head) // 3
+        order = head[turn:] + head[:turn]
+        if group >= 3:
+            order = order[:1] + order[:0:-1]
+        orders.append(order + tail)
     return orders
 
 
@@ -40,18 +44,29 @@
     return lax.dot_general(left, right, (dims, ((), ())), preferred_element_type=F32)
 
 
-def layer(peers, offsets, sizes, cols_ref, feat_ref, ws_ref, wn_ref, tiles_ref, pick_ref, flag_ref, cot_ref,
+def layer(peers, offsets, sizes, cols_ref, feat_hbm, ws_hbm, wn_hbm, tiles_hbm, pick_ref, flag_ref, cot_hbm,
           out_ref, gfeat_ref, res_ref, *scratch):
     steps = len(sizes) - 1
     (x, adj, inv, scat, going, halo, hub_out, hub_in, hub_all, pre, dpre, dneigh, own, back_out, back,
-     hback_out, hback, core_out, core_in, acc) = scratch[:20]
-    rs_out, rs_in = scratch[20:20 + steps], scratch[20 + steps:20 + 2 * steps]
+     hback_out, hback, core_out, core_in, acc, ws_ref, wn_ref, tiles_ref, cot_ref, fold_out, fold_in) = scratch[:26]
+    rs_out, rs_in = scratch[26:26 + steps], scratch[26 + steps:26 + 2 * steps]
     (halo_s, halo_r, hub_s, hub_r, back_s, back_r, hback_s, hback_r, core_s, core_r, rs_s, rs_r,
-     ag_s, ag_r, last_s, last_r) = scratch[20 + 2 * steps:]
+     ag_s, ag_r, last_s, last_r, load_s, quad_s, quad_r, fold_s, fold_r) = scratch[26 + 2 * steps:]
+    feat_ref = x.at[0]
+    loads = [
+        pltpu.make_async_copy(source, target, load_s.at[i])
+        for i, (source, target) in enumerate(
+            [(feat_hbm, feat_ref), (tiles_hbm, tiles_ref), (ws_hbm, ws_ref), (wn_hbm, wn_ref), (cot_hbm, cot_ref)]
+        )
+    ]
+    for load in loads:
+        load.start()
+    seat = lax.axis_index("dom") % QUAD
+    far = peers // QUAD
     me = lax.axis_index("dom")
     core = me % 2
     mate = me + 1 - 2 * core
-    rows, width = feat_ref.shape
+    rows, width = x.shape[1:]
     hid = ws_ref.shape[1]
     row_blocks, slots, tile, _ = tiles_ref.shape
     col_blocks = adj.shape[1] // tile
@@ -74,11 +89,11 @@
 
     picks = pick_ref.shape[1]
     scat[...] = (lax.broadcasted_iota(jnp.int32, (rows, picks), 0) == pick_ref[...]).astype(F32).astype(BF16)
-    x[0] = feat_ref[...]
+    loads[0].wait()
     picked = dot(scat[...], feat_ref[...], ((0,), (0,)))
     going[...] = picked[:caps].astype(BF16)
     hub_out[...] = picked[caps:caps + 4]
-    hub_in[me] = picked[caps:caps + 4]
+    hub_in[me // QUAD] = picked[caps:caps + 4]
     pl.semaphore_wait(barrier, peers - 1)
 
     part = caps // len(offsets)
@@ -89,7 +104,16 @@
                       lax.rem(me + offsets[q] + peers, peers))
 
     def hub_copy(k):
-        return remote(hub_out, hub_in.at[me], hub_s.at[k], hub_r.at[k], lax.rem(me + k, peers))
+        return remote(hub_out, hub_in.at[me // QUAD], hub_s.at[k], hub_r.at[k], lax.rem(me + QUAD * k, peers))
+
+    def mate_of(k):
+        return me - seat + (seat + k) % QUAD
+
+    def quad_copy(k):
+        return remote(hub_all.at[seat], hub_all.at[seat], quad_s.at[k], quad_r.at[k], mate_of(k))
+
+    def fold_copy(k):
+        return remote(fold_out.at[(seat + k) % QUAD], fold_in.at[seat], fold_s.at[k], fold_r.at[k], mate_of(k))
 
     def back_copy(q):
         piece = pl.ds(q * part, part)
@@ -97,26 +121,26 @@
                       lax.rem(me - offsets[q] + peers, peers))
 
     def hback_copy(k):
-        peer = lax.rem(me + k, peers)
-        return remote(hback_out.at[peer], hback.at[me], hback_s.at[k], hback_r.at[k], peer)
+        peer = lax.rem(me + QUAD * k, peers)
+        return remote(hback_out.at[peer // QUAD], hback.at[me // QUAD], hback_s.at[k], hback_r.at[k], peer)
 
     def start_all(make):
         def body(k, carry):
             make(k).start()
             return carry
-        lax.fori_loop(1, peers, body, 0)
+        lax.fori_loop(1, far, body, 0)
 
     def wait_recv_all(make):
         def body(k, carry):
             make(k).wait_recv()
             return carry
-        lax.fori_loop(1, peers, body, 0)
+        lax.fori_loop(1, far, body, 0)
 
     def wait_send_all(make):
         def body(k, carry):
             make(k).wait_send()
             return carry
-        lax.fori_loop(1, peers, body, 0)
+        lax.fori_loop(1, far, body, 0)
 
     start_all(hub_copy)
     for q in range(len(offsets)):
@@ -136,7 +160,18 @@
             adj[at, t * tile:(t + 1) * tile] = total.astype(BF16)
         return carry
 
+    loads[1].wait()
     lax.fori_loop(0, row_blocks, build, 0)
+    hubs = peers * 4
+    made = lax.broadcasted_iota(jnp.int32, (hubs, hubs), 0)
+    wanted = (made // 4) % QUAD * peers + made // (4 * QUAD) * 4 + made % 4
+    turned = (lax.broadcasted_iota(jnp.int32, (hubs, hubs), 1) == wanted).astype(F32).astype(BF16)
+    adj[:, rows + caps:] = dot(adj[:, rows + caps:], turned).astype(BF16)
+    wait_recv_all(hub_copy)
+    hub_all[seat] = jnp.concatenate([hub_in[j] for j in range(far)], axis=0).astype(BF16)
+    for k in range(1, QUAD):
+        quad_copy(k).start()
+    loads[2].wait()
     half = rows // 2
     for r in range(2):
         at = slice(r * half, (r + 1) * half)
@@ -145,13 +180,14 @@
 
     for q in range(len(offsets)):
         halo_copy(q).wait_recv()
-    wait_recv_all(hub_copy)
-    for j in range(0, peers, 4):
-        hub_all[4 * j:4 * j + 16] = jnp.concatenate([hub_in[j + i] for i in range(4)], axis=0).astype(BF16)
+    for k in range(1, QUAD):
+        quad_copy(k).wait_recv()
+    loads[3].wait()
+    loads[4].wait()
 
     for r in range(2):
         at = slice(r * half, (r + 1) * half)
-        total = own[at] + dot(adj[at, rows:rows + caps], halo[...]) + dot(adj[at, rows + caps:], hub_all[...])
+        total = own[at] + dot(adj[at, rows:rows + caps], halo[...]) + dot(adj[at, rows + caps:], hub_all[...].reshape(hubs, width))
         neigh = (total * inv[at]).astype(BF16)
         x[1, at] = neigh
         whole = pre[at] + dot(neigh, wn_ref[...])
@@ -162,11 +198,15 @@
     def core_copy(g):
         return remote(core_out.at[g], core_in.at[g], core_s.at[g], core_r.at[g], mate)
 
-    for g in range(GROUPS):
-        core_out[g] = dot(x[1 - core, :, g * grows:(g + 1) * grows], dpre[...], ((0,), (0,))).astype(BF16)
-        core_copy(g).start()
-    for g in range(GROUPS):
-        acc[g] = dot(x[core, :, g * grows:(g + 1) * grows], dpre[...], ((0,), (0,)))
+    for g in range(0, GROUPS, 2):
+        term = dot(x[1 - core, :, g * grows:(g + 2) * grows], dpre[...], ((0,), (0,))).astype(BF16)
+        for i in range(2):
+            core_out[g + i] = term[i * grows:(i + 1) * grows]
+            core_copy(g + i).start()
+    for g in range(0, GROUPS, 2):
+        term = dot(x[core, :, g * grows:(g + 2) * grows], dpre[...], ((0,), (0,)))
+        for i in range(2):
+            acc[g + i] = term[i * grows:(i + 1) * grows]
 
     zero = me * 0
     places = [(zero, zero)] * GROUPS
@@ -229,13 +269,12 @@
         at = slice(r * half, (r + 1) * half)
         dneigh[at] = (dot(dpre[at], wn_ref[...], ((1,), (1,))) * inv[at]).astype(BF16)
     back_out[...] = dot(adj[:, rows:rows + caps], dneigh[...], ((0,), (0,))).astype(BF16)
-    hubs = dot(adj[:, rows + caps:], dneigh[...], ((0,), (0,)))
-    for j in range(peers):
-        hback_out[j] = hubs[4 * j:4 * j + 4]
-    hback[me] = hback_out[me]
     for q in range(len(offsets)):
         back_copy(q).start()
-    start_all(hback_copy)
+    fold_out[...] = dot(adj[:, rows + caps:], dneigh[...], ((0,), (0,))).astype(BF16).reshape(QUAD, peers, width)
+    fold_in[seat] = fold_out[seat]
+    for k in range(1, QUAD):
+        fold_copy(k).start()
 
     for s in range(steps):
         for g in range(GROUPS):
@@ -250,7 +289,15 @@
             for r in range(2):
                 at = slice(r * half, (r + 1) * half)
                 own[at] = dot(dpre[at], ws_ref[...], ((1,), (1,)))
+        elif s == 1:
             own[...] += dot(adj[:, :rows], dneigh[...], ((0,), (0,)))
+            for k in range(1, QUAD):
+                fold_copy(k).wait_recv()
+            fold = jnp.sum(fold_in[...].astype(F32), axis=0)
+            for j in range(far):
+                hback_out[j] = fold[4 * j:4 * j + 4]
+            hback[me // QUAD] = hback_out[me // QUAD]
+            start_all(hback_copy)
 
     for s in reversed(range(steps)):
         for g in range(GROUPS):
@@ -278,6 +325,9 @@
     for q in range(len(offsets)):
         halo_copy(q).wait_send()
         back_copy(q).wait_send()
+    for k in range(1, QUAD):
+        quad_copy(k).wait_send()
+        fold_copy(k).wait_send()
     wait_send_all(hub_copy)
     wait_send_all(hback_copy)
     for g in range(GROUPS):
@@ -321,28 +371,37 @@
         vmem((caps, width), BF16),
         vmem((caps, width), BF16),
         vmem((4, width), F32),
-        vmem((peers, 4, width), F32),
-        vmem((hubs, width), BF16),
+        vmem((peers // QUAD, 4, width), F32),
+        vmem((QUAD, peers, width), BF16),
         vmem((rows, hid), F32),
         vmem((rows, hid), BF16),
         vmem((rows, width), BF16),
         vmem((rows, width), F32),
         vmem((caps, width), BF16),
         vmem((caps, width), BF16),
-        vmem((peers, 4, width), F32),
-        vmem((peers, 4, width), F32),
+        vmem((peers // QUAD, 4, width), F32),
+        vmem((peers // QUAD, 4, width), F32),
         vmem((GROUPS, grows, hid), BF16),
         vmem((GROUPS, grows, hid), BF16),
         vmem((GROUPS, grows, hid), F32),
+        vmem(w_self.shape, BF16),
+        vmem(w_neigh.shape, BF16),
+        vmem(tile_weights.shape, tile_weights.dtype),
+        vmem(cotangent.shape, BF16),
+        vmem((QUAD, peers, width), BF16),
+        vmem((QUAD, peers, width), BF16),
     ]
     scratch += [vmem((GROUPS, *sizes[s + 1]), BF16) for s in range(steps)] * 2
     q = len(offsets)
+    far = peers // QUAD
     scratch += [
-        dma((q,)), dma((q,)), dma((peers,)), dma((peers,)), dma((q,)), dma((q,)), dma((peers,)), dma((peers,)),
+        dma((q,)), dma((q,)), dma((far,)), dma((far,)), dma((q,)), dma((q,)), dma((far,)), dma((far,)),
         dma((GROUPS,)), dma((GROUPS,)), dma((steps, GROUPS)), dma((steps, GROUPS)),
         dma((steps, GROUPS)), dma((steps, GROUPS)), dma((GROUPS,)), dma((GROUPS,)),
+        dma((5,)), dma((QUAD,)), dma((QUAD,)), dma((QUAD,)), dma((QUAD,)),
     ]
     whole = pl.BlockSpec(memory_space=pltpu.VMEM)
+    anywhere = pl.BlockSpec(memory_space=pl.ANY)
     out_rows, grad, both = pl.pallas_call(
         functools.partial(layer, peers, offsets, sizes),
         out_shape=(
@@ -350,7 +409,7 @@
             jax.ShapeDtypeStruct((rows, width), BF16),
             jax.ShapeDtypeStruct((2, width, hid), BF16),
         ),
-        in_specs=[pl.BlockSpec(memory_space=pltpu.SMEM)] + [whole] * 7,
+        in_specs=[pl.BlockSpec(memory_space=pltpu.SMEM)] + [anywhere] * 4 + [whole] * 2 + [anywhere],
         out_specs=(whole,) * 3,
         scratch_shapes=scratch,
         compiler_params=pltpu.CompilerParams(

time: 94 us -> 79.4 us (0.84)
  Pallas kernels: 83.5 us -> 68.8 us
    pallas_call x1, Pallas kernels: 83.5 us -> 68.8 us  [on_device(): pl.pallas_call(functools.partial(layer, peers, offsets, sizes), out_shape...]
where the time goes in v2:
time: 79.4 us; the launch traced here: 79 us
  Pallas kernels  68.8 us (87%)
  other arithmetic  6.27 us (8%)
  local copies, waits for them, and re-layouts  3.26 us (4%)
    pallas_call x1, Pallas kernels, on_device(): pl.pallas_call(functools.partial(layer, peers, offsets, sizes), out_shape...  68.8 us
    convert_element_type x1, other arithmetic, on_device(): return (out_rows, grad, both[0].astype(F32), both[1].astype(F32))  5.46 us
    unnamed x6, local copies, waits for them, and re-layouts  1.86 us

profile of v2, /device:TPU:1, one launch (start us, length us, event | category | flops | bytes accessed | tf_op | source)
XLA Modules:
  0.0 79.0 jit_solution(4448495853258792257)
XLA Ops:
  0.6 0.8 %bitcast_select_fusion = s32[32,32]{1,0:T(8,128)S(1)} fusion(s32[1,32,32]{2,1,0:T(8,128)} %param.15, s32[32]{0:T(128)} %bitcast.28), kind=kLoop, calls=%fused_computation.5 | loop fusion | flops 2048 | bytes 8320 | tf_op jit(solution)/shard_map/jit(_where)/select_n | solution.py:351
  1.5 0.8 %concatenate.7 = s32[384]{0:T(512)S(1)} concatenate(s32[32]{0:T(128)S(1)} %get-tuple-element.21, s32[32]{0:T(128)S(1)} %get-tuple-element.20, s32[32]{0:T(128)S(1)} %get-tuple-element.19, s32[32]{0:T(128)S(1)} %get-tuple-element.18, s32[32]{0:T(128)S(1)} %get-tuple-element.17, s32[32]{0:T(128)S(1)} %get-tuple-element.16, s32[32]{0:T(128)S(1)} %get-tuple-element.15, ...), dimensions={0} | concatenate | bytes 3072 | tf_op jit(solution)/shard_map/concatenate | solution.py:358
  2.3 0.6 broadcast_in_dim.13.pick_ref
  2.9 68.8 %shard_map.129 = (bf16[512,1024]{1,0:T(8,128)(2,1)}, bf16[512,768]{1,0:T(8,128)(2,1)}, bf16[2,768,1024]{2,1,0:T(8,128)(2,1)}) custom-call(s32[4,6]{1,0:T(4,128)} %cols_ref.1, bf16[512,768]{1,0:T(8,128)(2,1)} %feat_hbm.1, bf16[768,1024]{1,0:T(8,128)(2,1)} %ws_hbm.1, bf16[768,1024]{1,0:T(8,128)(2,1)} %wn_hbm.1, s32[4,6,128,128]{3,2,1,0:T(8,128)} %tiles_hbm.1, ...), custom_call_target="tpu_custom_call" | custom-call | flops 6442450944 | bytes 12582912 | tf_op jit(solution)/shard_map/pallas_call | solution.py:405
  71.7 0.0 copy-start
  71.7 0.0 copy-start.1
  71.7 5.5 %bitcast_convert_fusion = (f32[768,1024]{1,0:T(8,128)}, f32[768,1024]{1,0:T(8,128)}) fusion(bf16[2,768,1024]{2,1,0:T(8,128)(2,1)} %get-tuple-element.9), kind=kLoop, calls=%fused_computation | loop fusion | flops 1572864 | bytes 9437184 | tf_op jit(solution)/shard_map/convert_element_type | solution.py:422
  77.2 0.0 copy-done
  77.2 1.0 %copy.16 = bf16[512,1024]{1,0:T(8,128)(2,1)} copy(bf16[512,1024]{1,0:T(8,128)(2,1)S(1)} %copy-done) | data formatting | bytes 2097152
  78.2 0.0 copy-done.1
  78.2 0.9 %copy.17 = bf16[512,768]{1,0:T(8,128)(2,1)} copy(bf16[512,768]{1,0:T(8,128)(2,1)S(1)} %copy-done.1) | data formatting | bytes 1572864
  (4 shorter events, 0.0 us)
Async XLA Ops:
  71.7 5.5 %copy-start = (bf16[512,1024]{1,0:T(8,128)(2,1)S(1)}, bf16[512,1024]{1,0:T(8,128)(2,1)}, u32[]{:S(2)}) copy-start(bf16[512,1024]{1,0:T(8,128)(2,1)} %get-tuple-element.26) | copy-start | bytes 3145732
  71.7 6.4 %copy-start.1 = (bf16[512,768]{1,0:T(8,128)(2,1)S(1)}, bf16[512,768]{1,0:T(8,128)(2,1)}, u32[]{:S(2)}) copy-start(bf16[512,768]{1,0:T(8,128)(2,1)} %get-tuple-element.27) | copy-start | bytes 2359300

commit v3 on v2

--- a/solution.py
+++ b/solution.py
@@ -44,14 +44,16 @@
     return lax.dot_general(left, right, (dims, ((), ())), preferred_element_type=F32)
 
 
-def layer(peers, offsets, sizes, cols_ref, feat_hbm, ws_hbm, wn_hbm, tiles_hbm, pick_ref, flag_ref, cot_hbm,
-          out_ref, gfeat_ref, res_ref, *scratch):
+def layer(peers, offsets, sizes, cols_ref, count_ref, hubrow_ref, feat_hbm, ws_hbm, wn_hbm, tiles_hbm, sends_ref,
+          flag_ref, cot_hbm,
+          out_hbm, gfeat_ref, res_hbm, *scratch):
     steps = len(sizes) - 1
     (x, adj, inv, scat, going, halo, hub_out, hub_in, hub_all, pre, dpre, dneigh, own, back_out, back,
-     hback_out, hback, core_out, core_in, acc, ws_ref, wn_ref, tiles_ref, cot_ref, fold_out, fold_in) = scratch[:26]
-    rs_out, rs_in = scratch[26:26 + steps], scratch[26 + steps:26 + 2 * steps]
+     hback_out, hback, core_out, core_in, acc, ws_ref, wn_ref, tiles_ref, cot_ref, fold_out, fold_in,
+     pick_ref, out_ref, res_ref) = scratch[:29]
+    rs_out, rs_in = scratch[29:29 + steps], scratch[29 + steps:29 + 2 * steps]
     (halo_s, halo_r, hub_s, hub_r, back_s, back_r, hback_s, hback_r, core_s, core_r, rs_s, rs_r,
-     ag_s, ag_r, last_s, last_r, load_s, quad_s, quad_r, fold_s, fold_r) = scratch[26 + 2 * steps:]
+     ag_s, ag_r, last_s, last_r, load_s, quad_s, quad_r, fold_s, fold_r, store_s) = scratch[29 + 2 * steps:]
     feat_ref = x.at[0]
     loads = [
         pltpu.make_async_copy(source, target, load_s.at[i])
@@ -88,6 +90,16 @@
     lax.fori_loop(1, peers, greet, 0)
 
     picks = pick_ref.shape[1]
+    cap = sends_ref.shape[2]
+    for q, offset in enumerate(offsets):
+        peer = lax.rem(me + offset + peers, peers)
+        live = lax.broadcasted_iota(jnp.int32, (1, cap), 1) < count_ref[0, peer]
+        pick_ref[:, q * cap:(q + 1) * cap] = jnp.where(live, sends_ref[0, pl.ds(peer, 1), :], -1)
+    lane = lax.broadcasted_iota(jnp.int32, (1, picks - caps), 1)
+    extra = jnp.full((1, picks - caps), -1, jnp.int32)
+    for i in range(4):
+        extra = jnp.where((lane == i) | (lane == i + 4), hubrow_ref[0, i], extra)
+    pick_ref[:, caps:] = extra
     scat[...] = (lax.broadcasted_iota(jnp.int32, (rows, picks), 0) == pick_ref[...]).astype(F32).astype(BF16)
     loads[0].wait()
     picked = dot(scat[...], feat_ref[...], ((0,), (0,)))
@@ -195,6 +207,9 @@
         out_ref[at] = (whole * sigma).astype(BF16)
         dpre[at] = (cot_ref[at].astype(F32) * sigma * (1.0 + whole * (1.0 - sigma))).astype(BF16)
 
+    out_store = pltpu.make_async_copy(out_ref, out_hbm, store_s.at[2 * GROUPS])
+    out_store.start()
+
     def core_copy(g):
         return remote(core_out.at[g], core_in.at[g], core_s.at[g], core_r.at[g], mate)
 
@@ -255,6 +270,10 @@
         size = sizes[s + 1]
         spot = res_ref.at[(core, *ds(row + g * grows, col, size))]
         return remote(spot, spot, ag_s.at[s, g], ag_r.at[s, g], me + step - 2 * step * bit)
+
+    def store(side, g):
+        spot = (core if side == 0 else 1 - core, pl.ds(g * grows, grows))
+        return pltpu.make_async_copy(res_ref.at[spot], res_hbm.at[spot], store_s.at[side * GROUPS + g])
 
     def last_copy(g):
         spot = res_ref.at[core, pl.ds(g * grows, grows)]
@@ -306,6 +325,7 @@
                 ag_copy(s - 1, g).start()
             else:
                 last_copy(g).start()
+                store(0, g).start()
 
     for q in range(len(offsets)):
         back_copy(q).wait_recv()
@@ -322,6 +342,8 @@
 
     for g in range(GROUPS):
         last_copy(g).wait_recv()
+        store(1, g).start()
+    out_store.wait()
     for q in range(len(offsets)):
         halo_copy(q).wait_send()
         back_copy(q).wait_send()
@@ -332,6 +354,8 @@
     wait_send_all(hback_copy)
     for g in range(GROUPS):
         core_copy(g).wait_send()
+        store(0, g).wait()
+        store(1, g).wait()
         last_copy(g).wait_send()
         for s in range(steps):
             rs_copy(s, g).wait_send()
@@ -340,7 +364,6 @@
 
 def on_device(peers, features, w_self, w_neigh, tile_cols, tile_weights, send_rows, send_counts, hub_rows, readers,
               cotangent):
-    me = lax.axis_index("dom")
     rows, width = features.shape
     hid = w_self.shape[1]
     cap = send_rows.shape[2]
@@ -348,15 +371,7 @@
     caps = len(offsets) * cap
     hubs = readers.shape[1]
     tile = tile_weights.shape[2]
-    targets = jnp.where(
-        jnp.arange(cap, dtype=jnp.int32)[None, :] < send_counts[0][:, None], send_rows[0], -1
-    )
-    wrapped = jnp.concatenate([targets[-REACH:], targets, targets[:REACH]], axis=0)
-    window = lax.dynamic_slice_in_dim(wrapped, me, 2 * REACH + 1, 0)
-    lists = [window[REACH + offset] for offset in offsets]
-    spare = jnp.full((tile - 2 * hub_rows.shape[1],), -1, jnp.int32)
-    pick = jnp.concatenate(lists + [hub_rows[0], hub_rows[0], spare])[None, :]
-    picks = pick.shape[1]
+    picks = caps + tile
 
     steps = peers.bit_length() - 2
     grows = width // GROUPS
@@ -390,6 +405,9 @@
         vmem(cotangent.shape, BF16),
         vmem((QUAD, peers, width), BF16),
         vmem((QUAD, peers, width), BF16),
+        vmem((1, picks), jnp.int32),
+        vmem((rows, hid), BF16),
+        vmem((2, width, hid), BF16),
     ]
     scratch += [vmem((GROUPS, *sizes[s + 1]), BF16) for s in range(steps)] * 2
     q = len(offsets)
@@ -398,10 +416,10 @@
         dma((q,)), dma((q,)), dma((far,)), dma((far,)), dma((q,)), dma((q,)), dma((far,)), dma((far,)),
         dma((GROUPS,)), dma((GROUPS,)), dma((steps, GROUPS)), dma((steps, GROUPS)),
         dma((steps, GROUPS)), dma((steps, GROUPS)), dma((GROUPS,)), dma((GROUPS,)),
-        dma((5,)), dma((QUAD,)), dma((QUAD,)), dma((QUAD,)), dma((QUAD,)),
+        dma((5,)), dma((QUAD,)), dma((QUAD,)), dma((QUAD,)), dma((QUAD,)), dma((2 * GROUPS + 1,)),
     ]
     whole = pl.BlockSpec(memory_space=pltpu.VMEM)
-    anywhere = pl.BlockSpec(memory_space=pl.ANY)
+    anywhere = pl.BlockSpec(memory_space=pltpu.HBM)
     out_rows, grad, both = pl.pallas_call(
         functools.partial(layer, peers, offsets, sizes),
         out_shape=(
@@ -409,8 +427,8 @@
             jax.ShapeDtypeStruct((rows, width), BF16),
             jax.ShapeDtypeStruct((2, width, hid), BF16),
         ),
-        in_specs=[pl.BlockSpec(memory_space=pltpu.SMEM)] + [anywhere] * 4 + [whole] * 2 + [anywhere],
-        out_specs=(whole,) * 3,
+        in_specs=[pl.BlockSpec(memory_space=pltpu.SMEM)] * 3 + [anywhere] * 4 + [whole] * 2 + [anywhere],
+        out_specs=(anywhere, whole, anywhere),
         scratch_shapes=scratch,
         compiler_params=pltpu.CompilerParams(
             collective_id=0, has_side_effects=True, vmem_limit_bytes=56 * 1024 * 1024
@@ -418,7 +436,7 @@
         cost_estimate=pl.CostEstimate(
             flops=8 * 2 * rows * width * hid, bytes_accessed=16 * rows * width * 2, transcendentals=rows * hid
         ),
-    )(tile_cols, features, w_self, w_neigh, tile_weights, pick, readers, cotangent)
+    )(tile_cols, send_counts, hub_rows, features, w_self, w_neigh, tile_weights, send_rows, readers, cotangent)
     return out_rows, grad, both[0].astype(F32), both[1].astype(F32)
 
 

time: 79.4 us -> 76.4 us (0.962)
  local copies, waits for them, and re-layouts: 3.26 us -> 1.86 us
  other arithmetic: 6.27 us -> 5.46 us
    concatenate x1 -> x0, local copies, waits for them, and re-layouts: 0.82 us -> none  [on_device(): pick = jnp.concatenate(lists + [hub_rows[0], hub_rows[0], spare])[None, :]]
where the time goes in v3:
time: 76.4 us; the launch traced here: 76.2 us
  Pallas kernels  68.2 us (89%)
  other arithmetic  5.46 us (7%)
  local copies, waits for them, and re-layouts  1.86 us (2%)
    pallas_call x1, Pallas kernels, on_device(): pl.pallas_call(functools.partial(layer, peers, offsets, sizes), out_shape...  68.2 us
    convert_element_type x1, other arithmetic, on_device(): return (out_rows, grad, both[0].astype(F32), both[1].astype(F32))  5.46 us
    unnamed x6, local copies, waits for them, and re-layouts  1.86 us

profile of v3, /device:TPU:1, one launch (start us, length us, event | category | flops | bytes accessed | tf_op | source)
XLA Modules:
  0.0 76.2 jit_solution(13672354047100036564)
XLA Ops:
  0.6 68.2 %shard_map.129 = (bf16[512,1024]{1,0:T(8,128)(2,1)}, bf16[512,768]{1,0:T(8,128)(2,1)}, bf16[2,768,1024]{2,1,0:T(8,128)(2,1)}) custom-call(s32[4,6]{1,0:T(4,128)} %cols_ref.1, s32[1,32]{1,0:T(1,128)} %count_ref.1, s32[1,4]{1,0:T(1,128)} %hubrow_ref.1, bf16[512,768]{1,0:T(8,128)(2,1)} %feat_hbm.1, bf16[768,1024]{1,0:T(8,128)(2,1)} %ws_hbm.1, ...), custom_call_target="tpu_custom_call" | custom-call | flops 6442450944 | bytes 12582912 | tf_op jit(solution)/shard_map/pallas_call | solution.py:423
  68.9 0.0 copy-start
  68.9 0.0 copy-start.1
  68.9 5.5 %bitcast_convert_fusion = (f32[768,1024]{1,0:T(8,128)}, f32[768,1024]{1,0:T(8,128)}) fusion(bf16[2,768,1024]{2,1,0:T(8,128)(2,1)} %get-tuple-element.9), kind=kLoop, calls=%fused_computation | loop fusion | flops 1572864 | bytes 9437184 | tf_op jit(solution)/shard_map/convert_element_type | solution.py:440
  74.3 0.0 copy-done
  74.4 1.0 %copy.16 = bf16[512,1024]{1,0:T(8,128)(2,1)} copy(bf16[512,1024]{1,0:T(8,128)(2,1)S(1)} %copy-done) | data formatting | bytes 2097152
  75.3 0.0 copy-done.1
  75.3 0.9 %copy.17 = bf16[512,768]{1,0:T(8,128)(2,1)} copy(bf16[512,768]{1,0:T(8,128)(2,1)S(1)} %copy-done.1) | data formatting | bytes 1572864
Async XLA Ops:
  68.9 5.5 %copy-start = (bf16[512,1024]{1,0:T(8,128)(2,1)S(1)}, bf16[512,1024]{1,0:T(8,128)(2,1)}, u32[]{:S(2)}) copy-start(bf16[512,1024]{1,0:T(8,128)(2,1)} %get-tuple-element.16) | copy-start | bytes 3145732
  68.9 6.4 %copy-start.1 = (bf16[512,768]{1,0:T(8,128)(2,1)S(1)}, bf16[512,768]{1,0:T(8,128)(2,1)}, u32[]{:S(2)}) copy-start(bf16[512,768]{1,0:T(8,128)(2,1)} %get-tuple-element.17) | copy-start | bytes 2359300
